TPU v7x, 512 devices: a whole 4x4x16 slice. The times are simulated.
512 devices in a mesh: section: 4 (over y), task: 32 (over z, core), row: 4 (over x).
Axes of the slice: x: 4, y: 4, z: 16, core: 2. Of those that a mesh axis runs over, the one named last changes fastest.
Arguments:
- hidden: bfloat16 [4096, 5120], P(('section', 'row'), 'task'), may hold values from -6 to 6
- piece_weight: bfloat16 [5120, 4096], P('task'), may hold values from -0.078125 to 0.078125
- task_embed: bfloat16 [8192, 512], P('task'), may hold values from -0.25 to 0.25
- task_bias: float32 [8192, 8], P('task'), may hold values from -4 to 4
- event_bin: int32 [4096, 8192], P(('section', 'row'), 'task'), may hold values from 0 to 7
- censored: int32 [4096, 8192], P(('section', 'row'), 'task'), may hold values 0 or 1
- patient_id: int32 [4096], P(('section', 'row')), may hold values from 0 to 255
- patient_rows: int32 [256], replicated, may hold values from 1 to 9
Outputs:
- hidden_grad: bfloat16 [4096, 5120], P(('section', 'row'), 'task')
- task_grad: float32 [8192, 512], P('task')
- loss: float32 [], replicated
All inputs are finite; a program needn't handle non-finite values. No bound on the sum of `censored` on one device may be relied on, other than what follows from the above.
Results may differ from a plain program's by a relative error of at most 0.025.
Values may be sent and summed in bfloat16 or wider, within the bound.
A program may use at most 64 MiB of HBM per device.

v0:
```python
import functools

import jax
import jax.numpy as jnp
from jax import lax
from jax.experimental import pallas as pl
from jax.experimental.pallas import tpu as pltpu
from jax.sharding import PartitionSpec as P

MESH = pl.DeviceIdType.MESH
F32 = jnp.float32
BF16 = jnp.bfloat16
LANES = 128
STREAMS = 2
CHAIN = (2, 4, 6, 8)
NT = (((1,), (1,)), ((), ()))
TN = (((0,), (0,)), ((), ()))


def kernel(
    loss_scale,
    grad_scale,
    hid_hbm,
    pw_hbm,
    te_hbm,
    bias_hbm,
    bins_hbm,
    cens_hbm,
    pid_hbm,
    prow_hbm,
    hg_out,
    tg_out,
    loss_out,
    pid_ref,
    prow_ref,
    hid,
    hid_rows,
    pw,
    te,
    bias,
    bins,
    cens,
    wrow,
    part,
    rs_out,
    rs_in,
    zbuf,
    pgf,
    gbuf,
    loss_acc,
    loss_x,
    loss_y,
    loss_pair,
    tg_acc,
    tg_send,
    tg_recv,
    tx_send,
    tx_recv,
    ty_send,
    ty_recv,
    tg_fin,
    acc_own,
    acc_sib,
    hg_send,
    hg_recv,
    send_sem,
    recv_sem,
    local_sem,
    pair_send,
    pair_recv,
    pw_send,
    pw_recv,
    px_send,
    px_recv,
    py_send,
    py_recv,
):
    rows = hid.shape[2]
    half_cols = pw.shape[2]
    tasks = te.shape[1]
    nz = part.shape[0]
    far = nz // 2
    pieces = half_cols // te.shape[2]
    per_piece = nz // pieces
    rb = rows // STREAMS
    nx = lax.axis_size("row")
    ny = lax.axis_size("section")
    task = lax.axis_index("task")
    x = lax.axis_index("row")
    y = lax.axis_index("section")
    z = task // 2
    core = task % 2
    sib = z * 2 + 1 - core

    def wrap(v):
        return (v + 2 * nz) % nz

    def z_dev(off):
        return wrap(z + off) * 2 + core

    def copy_to(src, dst, ss, rs, **where):
        return pltpu.make_async_remote_copy(
            src_ref=src,
            dst_ref=dst,
            send_sem=ss,
            recv_sem=rs,
            device_id=where,
            device_id_type=MESH,
        )

    mine = pl.ds(pl.multiple_of(core * half_cols, half_cols), half_cols)
    loads = [
        (hid_hbm, hid.at[0]),
        (pw_hbm.at[:, mine], pw.at[0]),
        (te_hbm, te.at[0]),
        (bias_hbm, bias.at[0]),
        (bins_hbm, bins.at[0]),
        (cens_hbm, cens.at[0]),
        (pid_hbm, pid_ref),
        (prow_hbm, prow_ref),
    ]
    loads = [pltpu.make_async_copy(a, b, local_sem.at[i]) for i, (a, b) in enumerate(loads)]
    for load in loads[:2]:
        load.start()

    barrier = pltpu.get_barrier_semaphore()
    strides = sorted({b - a for a, b in zip((0,) + CHAIN, CHAIN)} | {1})
    peers = [dict(task=sib)] + [dict(task=z_dev(s * n)) for n in strides for s in (1, -1)]
    peers += [dict(row=(x + j) % nx) for j in range(1, nx)]
    peers += [dict(section=(y + j) % ny) for j in range(1, ny)]
    for peer in peers:
        pl.semaphore_signal(barrier, inc=1, device_id=peer, device_id_type=MESH)
    pl.semaphore_wait(barrier, len(peers))

    pair = [
        (hid_hbm, hid.at[1]),
        (te_hbm, te.at[1]),
        (bias_hbm, bias.at[1]),
        (bins_hbm, bins.at[1]),
        (cens_hbm, cens.at[1]),
    ]
    pair = [
        copy_to(a, b, pair_send.at[i], pair_recv.at[i], task=sib) for i, (a, b) in enumerate(pair)
    ]

    part_cols = half_cols // far

    def pw_copy(n):
        q = (wrap(z + far) // 2 + n + far) % far
        there = pl.ds(
            pl.multiple_of((1 - core) * half_cols + q * part_cols, part_cols), part_cols
        )
        here = pl.ds(pl.multiple_of(q * part_cols, part_cols), part_cols)
        return copy_to(
            pw_hbm.at[:, there], pw.at[1, :, here], pw_send.at[q], pw_recv.at[q], task=sib
        )

    pw_order = [0] + [s * n for n in range(1, far // 2) for s in (1, -1)] + [far // 2]
    pair[0].start()
    for n in pw_order[:5]:
        pw_copy(n).start()
    for load in loads[2:]:
        load.start()

    def long_way(st):
        return 0 if st < STREAMS // 2 else 1

    def stops(d, st):
        return [c for c in CHAIN if c < far or d == long_way(st)]

    def before(off):
        return max([0] + [c for c in CHAIN if c < off])

    def behind(stop, d, st):
        last = far if d == long_way(st) else far - 1
        found = [off for off in range(1, last + 1) if before(off) == stop]
        return sorted(found, key=lambda off: off not in CHAIN)

    def sides(st):
        return (long_way(st), 1 - long_way(st))

    def rs_copy(ph, d, st, off):
        span = pl.ds(st * rb, rb)
        return copy_to(
            rs_out.at[ph, d, off - 1, span, :],
            rs_in.at[ph, d, off - 1, span, :],
            send_sem.at[2 * ph, d, st, off - 1],
            recv_sem.at[2 * ph, d, st, off - 1],
            task=z_dev((1 - 2 * d) * (off - before(off))),
        )

    def cols(c):
        return pl.ds(pl.multiple_of(c * LANES, LANES), LANES)

    def fill(k):
        stop = ([0] + list(CHAIN))[-1 - k]
        for off in [stop] + list(range(before(stop) + 1, stop)):
            chunks = [wrap(z + off)] if off in (0, far) else [wrap(z - off), wrap(z + off)]
            total = None
            for h in range(2):
                w = jnp.concatenate([pw[h, :, cols(c)] for c in chunks], axis=1)
                dots = jnp.dot(hid_rows[h], w, preferred_element_type=F32)
                total = dots if total is None else total + dots
            for i, c in enumerate(chunks):
                part[c] = total[:, i * LANES : (i + 1) * LANES]

    def rs_send(ph, d, st, off):
        span = pl.ds(st * rb, rb)
        total = part[wrap(z + (1 - 2 * d) * off), span, :]
        if off in stops(d, st):
            for other in behind(off, d, st):
                rs_copy(ph, d, st, other).wait_recv()
                total += rs_in[ph, d, other - 1, span, :].astype(F32)
        rs_out[ph, d, off - 1, span, :] = total.astype(BF16)
        rs_copy(ph, d, st, off).start()

    def rs_total(ph, st):
        span = pl.ds(st * rb, rb)
        total = part[z, span, :]
        for d in sides(st):
            for other in behind(0, d, st):
                rs_copy(ph, d, st, other).wait_recv()
                total += rs_in[ph, d, other - 1, span, :].astype(F32)
        return total

    def rs_chain(ph, st, k):
        stop = ([0] + list(CHAIN))[-1 - k]
        for d in sides(st):
            if k == 0:
                rs_send(ph, d, st, far if d == long_way(st) else far - 1)
            elif stop != far - 1 or d == long_way(st):
                rs_send(ph, d, st, stop)
        if k == 0:
            rs_leaves(ph, st, 0)

    def rs_leaves(ph, st, k):
        stop = ([0] + list(CHAIN))[-1 - k]
        for off in range(stop - 1, before(stop), -1):
            for d in sides(st):
                if off != far - 1 or d == long_way(st):
                    rs_send(ph, d, st, off)

    def rs_sent(ph, st):
        for d in range(2):
            for off in range(1, far + 1 if d == long_way(st) else far):
                rs_copy(ph, d, st, off).wait_send()

    def ag_copy(ph, d, st, off):
        buf = zbuf if ph == 0 else pgf
        extra = 16 if ph == 1 and st == STREAMS - 1 else 0
        sgn = 1 - 2 * d
        ref = buf.at[wrap(z - sgn * before(off)), pl.ds(st * rb, rb + extra), :]
        return copy_to(
            ref,
            ref,
            send_sem.at[2 * ph + 1, d, st, off - 1],
            recv_sem.at[2 * ph + 1, d, st, off - 1],
            task=z_dev(sgn * (off - before(off))),
        )

    def ag_arrived(ph, d, st, off):
        buf = zbuf if ph == 0 else pgf
        extra = 16 if ph == 1 and st == STREAMS - 1 else 0
        sgn = 1 - 2 * d
        if off < far or d == long_way(st):
            ref = buf.at[wrap(z - sgn * off), pl.ds(st * rb, rb + extra), :]
            copy_to(
                ref,
                ref,
                send_sem.at[2 * ph + 1, d, st, off - 1],
                recv_sem.at[2 * ph + 1, d, st, off - 1],
                task=z_dev(sgn * (off - before(off))),
            ).wait_recv()

    def ag_chain(ph, st, k):
        stop = ([0] + list(CHAIN))[k]
        for d in sides(st):
            if k > 0:
                ag_arrived(ph, d, st, stop)
            for off in behind(stop, d, st)[:1]:
                ag_copy(ph, d, st, off).start()

    def ag_leaves(ph, st, k):
        stop = ([0] + list(CHAIN))[k]
        for d in sides(st):
            for off in behind(stop, d, st)[1:]:
                ag_copy(ph, d, st, off).start()

    def ag_sent(ph, st, first, last):
        for d in range(2):
            for off in range(first, last + 1):
                if off < far or d == long_way(st):
                    ag_copy(ph, d, st, off).wait_send()

    between = [off for off in range(1, far) if off not in CHAIN]

    def prepare():
        loads[6].wait()
        loads[7].wait()
        ids = jnp.broadcast_to(pid_ref[...].astype(F32), (prow_ref.shape[1], rows)).T
        lane = lax.broadcasted_iota(jnp.int32, ids.shape, 1).astype(F32)
        record = jnp.where(ids == lane, prow_ref[...].astype(F32), 0.0)
        weight = 1.0 / jnp.sum(record, axis=1, keepdims=True)
        wrow[...] = jnp.broadcast_to(weight, wrow.shape)
        loss_acc[...] = jnp.zeros_like(loss_acc)
        tg_acc[...] = jnp.zeros_like(tg_acc)
        acc_own[...] = jnp.zeros_like(acc_own)
        acc_sib[...] = jnp.zeros_like(acc_sib)

    late = (wrap(z + far + 1) // per_piece) % pieces

    def head(st, first, last):
        span = pl.ds(st * rb, rb)
        order = [(late + 1 + i) % pieces for i in range(first, last)]
        zs = jnp.concatenate(
            [
                jnp.concatenate(
                    [zbuf[p * per_piece + k, span, :] for k in range(per_piece)], axis=1
                )
                for p in order
            ],
            axis=0,
        )
        total = None
        for h in range(2):
            dots = lax.dot_general(zs, te[h], NT, preferred_element_type=F32)
            edge = bins[h, span, :]
            alive = (1 - cens[h, span, :]).astype(F32)
            weight = wrow[span, :]
            grads = []
            nll = None
            for i, p in enumerate(order):
                piece = core * pieces + p
                logits = dots[i * rb : (i + 1) * rb] + bias[h, pl.ds(piece, 1), :]
                hazard = jnp.exp(logits)
                at = edge == piece
                hazard = jnp.where(edge > piece, hazard, jnp.where(at, 0.5 * hazard, 0.0))
                event = jnp.where(at, alive, 0.0)
                term = hazard - event * logits
                nll = term if nll is None else nll + term
                grad = (weight * (hazard - event)).astype(BF16)
                gbuf[h, p, span, :] = grad
                grads.append(grad)
            nll = (weight * nll).reshape(rb // 8, 8, tasks).sum(axis=0)
            loss_acc[...] += nll
            grads = jnp.concatenate(grads, axis=0)
            dots = jnp.dot(grads, te[h], preferred_element_type=F32)
            total = dots if total is None else total + dots
        for i, p in enumerate(order):
            for k in range(per_piece):
                part[p * per_piece + k, span, :] = total[
                    i * rb : (i + 1) * rb, k * LANES : (k + 1) * LANES
                ]

    def x_copy(j, src, dst, k):
        return copy_to(
            src, dst, px_send.at[k, j - 1], px_recv.at[k, j - 1], row=(x + j) % nx
        )

    def y_copy(j, src, dst, k):
        return copy_to(
            src, dst, py_send.at[k, j - 1], py_recv.at[k, j - 1], section=(y + j) % ny
        )

    def loss_x_copy(j):
        return x_copy(j, loss_x.at[x], loss_x.at[x], 0)

    def loss_y_copy(j):
        return y_copy(j, loss_y.at[y], loss_y.at[y], 0)

    bx = tasks // nx
    by = bx // ny

    def tgx_copy(j):
        peer = (x + j) % nx
        src = tx_send.at[pl.ds(pl.multiple_of(peer * bx, bx), bx), :]
        return x_copy(j, src, tx_recv.at[j - 1], 1)

    def tgy_copy(j):
        peer = (y + j) % ny
        src = ty_send.at[pl.ds(pl.multiple_of(peer * by, by), by), :]
        return y_copy(j, src, ty_recv.at[j - 1], 1)

    def agy_copy(j):
        ref = tg_fin.at[pl.ds(pl.multiple_of(x * bx + y * by, by), by), :]
        return y_copy(j, ref, ref, 2)

    def agx_copy(j):
        ref = tg_fin.at[pl.ds(pl.multiple_of(x * bx, bx), bx), :]
        return x_copy(j, ref, ref, 2)

    tg_copy = copy_to(tg_send, tg_recv, pair_send.at[5], pair_recv.at[5], task=sib)

    def tg_piece(p):
        zp = jnp.concatenate([zbuf[p * per_piece + k] for k in range(per_piece)], axis=1)
        for h in range(2):
            tg_acc[h] += lax.dot_general(gbuf[h, p], zp, TN, preferred_element_type=F32)

    def loss_terms():
        own = sum(loss_y[i] for i in range(1, ny)) + loss_y[0]
        own = jnp.sum(jnp.sum(own, axis=0, keepdims=True), axis=1, keepdims=True)
        own = jnp.broadcast_to(own, (16, LANES))
        place = lax.broadcasted_iota(jnp.int32, own.shape, 1)
        place += LANES * lax.broadcasted_iota(jnp.int32, own.shape, 0)
        high = own.astype(BF16).astype(F32)
        rest = own - high
        middle = rest.astype(BF16).astype(F32)
        low = rest - middle
        terms = jnp.where(
            place == 0, high, jnp.where(place == 1, middle, jnp.where(place == 2, low, 0.0))
        )
        pgf[z, pl.ds(rows, 16), :] = terms.astype(BF16)

    def plane():
        loss_x[x] = loss_acc[:, :LANES] + loss_acc[:, LANES:]
        for j in range(1, nx):
            loss_x_copy(j).start()
        for p in range(pieces // 2):
            tg_piece(p)
        yield
        for p in range(pieces // 2, pieces):
            tg_piece(p)
        tg_send[...] = tg_acc[1].astype(BF16)
        tg_copy.start()
        for j in range(1, nx):
            loss_x_copy(j).wait()
        loss_y[y] = sum(loss_x[i] for i in range(1, nx)) + loss_x[0]
        for j in range(1, ny):
            loss_y_copy(j).start()
        yield
        tg_copy.wait()
        tg_acc[0] += tg_recv[...].astype(F32)
        tx_send[...] = tg_acc[0].astype(BF16)
        for j in range(1, nx):
            tgx_copy(j).start()
        for j in range(1, ny):
            loss_y_copy(j).wait()
        loss_terms()
        yield
        total = tg_acc[0, pl.ds(pl.multiple_of(x * bx, bx), bx), :]
        for j in range(1, nx):
            tgx_copy(j).wait()
            total += tx_recv[j - 1].astype(F32)
        tg_acc[0, pl.ds(0, bx), :] = total
        ty_send[...] = total.astype(BF16)
        for j in range(1, ny):
            tgy_copy(j).start()
        yield
        total = tg_acc[0, pl.ds(pl.multiple_of(y * by, by), by), :]
        for j in range(1, ny):
            tgy_copy(j).wait()
            total += ty_recv[j - 1].astype(F32)
        place = pl.ds(pl.multiple_of(x * bx + y * by, by), by)
        tg_fin[place, :] = (total * grad_scale).astype(BF16)
        for j in range(1, ny):
            agy_copy(j).start()
        yield
        for j in range(1, ny):
            agy_copy(j).wait_send()
            from_y = (y + ny - j) % ny
            ref = tg_fin.at[pl.ds(pl.multiple_of(x * bx + from_y * by, by), by), :]
            y_copy(j, ref, ref, 2).wait_recv()
        for j in range(1, nx):
            agx_copy(j).start()
        yield
        for j in range(1, nx):
            agx_copy(j).wait_send()
            from_x = (x + nx - j) % nx
            ref = tg_fin.at[pl.ds(pl.multiple_of(from_x * bx, bx), bx), :]
            x_copy(j, ref, ref, 2).wait_recv()
        tg_out[...] = tg_fin[...]

    def add_chunks(st, offs):
        span = pl.ds(st * rb, rb)
        chunks = [wrap(z + off) for off in offs]
        value = jnp.concatenate([pgf[c, span, :] for c in chunks], axis=1)
        for h, acc in ((0, acc_own), (1, acc_sib)):
            w = jnp.concatenate([pw[h, :, cols(c)] for c in chunks], axis=1)
            acc[:, span] += lax.dot_general(w, value, NT, preferred_element_type=F32)

    def hg_copy(st):
        return copy_to(
            hg_send.at[st], hg_recv.at[st], pair_send.at[6 + st], pair_recv.at[6 + st], task=sib
        )

    def pw_arrived(*order):
        for m in order:
            pw_copy(m).wait_recv()

    def stream(st):
        span = pl.ds(st * rb, rb)
        n = len(CHAIN)
        for k in range(n):
            rs_chain(0, st, k)
            yield
            if st == 0 and k == 0:
                for m in pw_order[5:]:
                    pw_copy(m).start()
                pw_arrived(2, -2)
                fill(1)
            if k < n - 1:
                rs_leaves(0, st, k + 1)
            yield
            if st == 0 and k < n - 1:
                pw_arrived(*{0: (3, -3), 1: (4,)}.get(k, ()))
                fill(k + 2)
            if st == 0 and k > 0:
                for copy in {1: pair[1:3], 2: pair[3:4], 3: pair[4:5]}[k]:
                    copy.start()
            yield
        zbuf[z, span, :] = rs_total(0, st).astype(BF16)
        for k in range(n):
            ag_chain(0, st, k)
            yield
            ag_leaves(0, st, k)
            yield
            if k == 1:
                rs_sent(0, st)
            if st == 0 and k == 2:
                for copy in pair:
                    copy.wait_send()
                for m in pw_order:
                    pw_copy(m).wait_send()
            if k == n - 1:
                if st == 0:
                    for i in range(1, 5):
                        loads[1 + i].wait()
                        pair[i].wait_recv()
                for off in between[:-1]:
                    for d in sides(st):
                        ag_arrived(0, d, st, off)
                head(st, 0, pieces // 2)
            yield
        ag_chain(0, st, n)
        for d in sides(st):
            ag_arrived(0, d, st, far - 1)
        head(st, pieces // 2, pieces)
        for k in range(n):
            rs_chain(1, st, k)
            yield
            if k < n - 1:
                rs_leaves(1, st, k + 1)
            yield
            if k == 1:
                ag_sent(0, st, 1, far)
            yield
        pgf[z, span, :] = rs_total(1, st).astype(BF16)
        for k in range(n + 1):
            ag_chain(1, st, k)
            yield
            ag_leaves(1, st, k)
            yield
            if k == 0:
                add_chunks(st, [0])
            else:
                offs = [CHAIN[k - 1]]
                for off in between:
                    if before(off) == ([0] + list(CHAIN))[k - 1]:
                        for d in sides(st):
                            ag_arrived(1, d, st, off)
                        offs.append(off)
                add_chunks(st, [s * off for off in offs for s in (1, -1) if s * off > -far])
            if k == 1:
                rs_sent(1, st)
            if k == n - 1:
                ag_sent(1, st, 1, CHAIN[n - 2])
            if k == n:
                hg_send[st] = acc_sib[:, span].astype(BF16)
                hg_copy(st).start()
            yield

    loads[0].wait()
    loads[1].wait()
    hid_rows[0] = hid[0].T
    pair[0].wait_recv()
    hid_rows[1] = hid[1].T
    pw_arrived(0, 1, -1)
    fill(0)
    head_slot = len(CHAIN) * 2
    last_slot = len(CHAIN) * 4
    running = [stream(st) for st in range(STREAMS)]
    beside = None
    for slot in range(last_slot + 1):
        for _ in range(3):
            for steps in running:
                next(steps)
        if slot == 0:
            prepare()
        if slot == head_slot:
            beside = plane()
        if beside is not None and next(beside, True):
            beside = None
    for steps in running:
        for _ in steps:
            pass
    if beside is not None:
        for _ in beside:
            pass

    total = pgf[0, pl.ds(rows, 16), :].astype(F32)
    for c in range(1, nz):
        total += pgf[c, pl.ds(rows, 16), :].astype(F32)
    loss_pair[core] = total
    ref = loss_pair.at[core]
    last = 6 + STREAMS
    loss_copy = copy_to(ref, ref, pair_send.at[last], pair_recv.at[last], task=sib)
    loss_copy.start()
    for st in range(STREAMS):
        ag_sent(1, st, CHAIN[-2] + 1, far)
    loss_copy.wait()
    total = loss_pair[0] + loss_pair[1]
    loss_out[0, 0] = jnp.sum(total) * loss_scale
    for st in range(STREAMS):
        span = pl.ds(st * rb, rb)
        hg_copy(st).wait()
        hg_out[:, span] = (acc_own[:, span] + hg_recv[st].astype(F32)).astype(BF16)


def shards(
    hidden, piece_weight, task_embed, task_bias, event_bin, censored, patient_id, patient_rows
):
    patients = patient_rows.shape[0]
    rows, depth = hidden.shape
    tasks, width = task_embed.shape
    pieces = task_bias.shape[1]
    n_task = lax.axis_size("task")
    nx, ny = lax.axis_size("row"), lax.axis_size("section")
    nz = n_task // 2
    half = pieces * width // 2
    bx = tasks // nx
    by = bx // ny
    vmem = pl.BlockSpec(memory_space=pltpu.VMEM)
    in_hbm = pl.BlockSpec(memory_space=pltpu.HBM)
    dma = pltpu.SemaphoreType.DMA
    hg, tg, loss = pl.pallas_call(
        functools.partial(kernel, 1.0 / (patients * tasks * n_task), 1.0 / patients),
        out_shape=(
            pltpu.VMEM((depth, rows), BF16),
            pltpu.VMEM((tasks, width), BF16),
            jax.ShapeDtypeStruct((1, 1), F32),
        ),
        in_specs=[in_hbm] * 8,
        out_specs=(vmem, vmem, pl.BlockSpec(memory_space=pltpu.SMEM)),
        scratch_shapes=[
            pltpu.VMEM((1, rows), jnp.int32),
            pltpu.VMEM((1, patients), jnp.int32),
            pltpu.VMEM((2, depth, rows), BF16),
            pltpu.VMEM((2, rows, depth), BF16),
            pltpu.VMEM((2, depth, half), BF16),
            pltpu.VMEM((2, tasks, width), BF16),
            pltpu.VMEM((2, pieces, tasks), F32),
            pltpu.VMEM((2, rows, tasks), jnp.int32),
            pltpu.VMEM((2, rows, tasks), jnp.int32),
            pltpu.VMEM((rows, tasks), F32),
            pltpu.VMEM((nz, rows, LANES), F32),
            pltpu.VMEM((2, 2, nz // 2, rows, LANES), BF16),
            pltpu.VMEM((2, 2, nz // 2, rows, LANES), BF16),
            pltpu.VMEM((nz, rows, LANES), BF16),
            pltpu.VMEM((nz, rows + 16, LANES), BF16),
            pltpu.VMEM((2, pieces // 2, rows, tasks), BF16),
            pltpu.VMEM((8, tasks), F32),
            pltpu.VMEM((nx, 8, LANES), F32),
            pltpu.VMEM((ny, 8, LANES), F32),
            pltpu.VMEM((2, 16, LANES), F32),
            pltpu.VMEM((2, tasks, width), F32),
            pltpu.VMEM((tasks, width), BF16),
            pltpu.VMEM((tasks, width), BF16),
            pltpu.VMEM((tasks, width), BF16),
            pltpu.VMEM((nx - 1, bx, width), BF16),
            pltpu.VMEM((bx, width), BF16),
            pltpu.VMEM((ny - 1, by, width), BF16),
            pltpu.VMEM((tasks, width), BF16),
            pltpu.VMEM((depth, rows), F32),
            pltpu.VMEM((depth, rows), F32),
            pltpu.VMEM((STREAMS, depth, rows // STREAMS), BF16),
            pltpu.VMEM((STREAMS, depth, rows // STREAMS), BF16),
            dma((4, 2, STREAMS, nz // 2)),
            dma((4, 2, STREAMS, nz // 2)),
            dma((8,)),
            dma((7 + STREAMS,)),
            dma((7 + STREAMS,)),
            dma((nz // 2,)),
            dma((nz // 2,)),
            dma((3, nx - 1)),
            dma((3, nx - 1)),
            dma((3, ny - 1)),
            dma((3, ny - 1)),
        ],
        compiler_params=pltpu.CompilerParams(
            collective_id=0, has_side_effects=True, vmem_limit_bytes=60 * 1024 * 1024
        ),
        cost_estimate=pl.CostEstimate(
            flops=2400000000, bytes_accessed=4000000, transcendentals=600000
        ),
    )(
        hidden.T,
        piece_weight,
        task_embed,
        task_bias.T,
        event_bin,
        censored,
        patient_id.reshape(1, rows),
        patient_rows.reshape(1, patients),
    )
    return hg.T, tg.astype(F32), loss.reshape(())


def solution(mesh):
    return jax.shard_map(
        shards,
        mesh=mesh,
        in_specs=(
            P(("section", "row"), "task"),
            P("task", None),
            P("task", None),
            P("task", None),
            P(("section", "row"), "task"),
            P(("section", "row"), "task"),
            P(("section", "row")),
            P(),
        ),
        out_specs=(P(("section", "row"), "task"), P("task", None), P()),
        check_vma=False,
    )
```

profile of v0, /device:TPU:1, one launch (start us, length us, event | category | flops | bytes accessed | tf_op | source)
XLA Modules:
  0.0 98.8 jit_solution(17630569736135558506)
XLA Ops:
  0.6 94.9 %shard_map.103 = (bf16[160,256]{1,0:T(8,128)(2,1)S(1)}, bf16[256,512]{1,0:T(8,128)(2,1)S(1)}, f32[1,1]{1,0:T(1,128)}) custom-call(bf16[160,256]{1,0:T(8,128)(2,1)} %bitcast.7, bf16[160,4096]{1,0:T(8,128)(2,1)} %pw_hbm.1, bf16[256,512]{1,0:T(8,128)(2,1)} %te_hbm.1, f32[8,256]{1,0:T(8,128)} %bitcast.8, s32[256,256]{1,0:T(8,128)} %bins_hbm.1, ...), custom_call_target="tpu_custom_call" | custom-call | flops 2400000000 | bytes 4000000 | tf_op jit(solution)/shard_map/pallas_call | solution.py:635
  95.6 0.6 copy.13
  96.2 0.9 convert_element_type.3
where the time goes:
time: 98.9 us; the launch traced here: 98.8 us
  Pallas kernels  94.9 us (96%)
  between operations  2.33 us (2%)
    pallas_call x1, Pallas kernels, shards(): pl.pallas_call(functools.partial(kernel, 1.0 / (patients * tasks * n_task...  94.9 us

commit v1 on v0

--- a/solution.py
+++ b/solution.py
@@ -308,10 +308,12 @@
         acc_sib[...] = jnp.zeros_like(acc_sib)
 
     late = (wrap(z + far + 1) // per_piece) % pieces
-
-    def head(st, first, last):
+    near = z // per_piece
+    aside = (2 * late + 3 - near + pieces) % pieces
+    rest = [(late + 3) % pieces, late]
+
+    def head(st, order):
         span = pl.ds(st * rb, rb)
-        order = [(late + 1 + i) % pieces for i in range(first, last)]
         zs = jnp.concatenate(
             [
                 jnp.concatenate(
@@ -415,27 +417,29 @@
         loss_x[x] = loss_acc[:, :LANES] + loss_acc[:, LANES:]
         for j in range(1, nx):
             loss_x_copy(j).start()
-        for p in range(pieces // 2):
-            tg_piece(p)
+        tg_piece(0)
         yield
-        for p in range(pieces // 2, pieces):
-            tg_piece(p)
-        tg_send[...] = tg_acc[1].astype(BF16)
-        tg_copy.start()
         for j in range(1, nx):
             loss_x_copy(j).wait()
         loss_y[y] = sum(loss_x[i] for i in range(1, nx)) + loss_x[0]
         for j in range(1, ny):
             loss_y_copy(j).start()
+        tg_piece(1)
+        yield
+        tg_piece(2)
+        for j in range(1, ny):
+            loss_y_copy(j).wait()
+        loss_terms()
+        yield
+        tg_piece(3)
+        tg_send[...] = tg_acc[1].astype(BF16)
+        tg_copy.start()
         yield
         tg_copy.wait()
         tg_acc[0] += tg_recv[...].astype(F32)
         tx_send[...] = tg_acc[0].astype(BF16)
         for j in range(1, nx):
             tgx_copy(j).start()
-        for j in range(1, ny):
-            loss_y_copy(j).wait()
-        loss_terms()
         yield
         total = tg_acc[0, pl.ds(pl.multiple_of(x * bx, bx), bx), :]
         for j in range(1, nx):
@@ -521,20 +525,24 @@
                     copy.wait_send()
                 for m in pw_order:
                     pw_copy(m).wait_send()
-            if k == n - 1:
+            if k == n - 2:
                 if st == 0:
                     for i in range(1, 5):
                         loads[1 + i].wait()
                         pair[i].wait_recv()
-                for off in between[:-1]:
+                for off in between[:-2]:
                     for d in sides(st):
                         ag_arrived(0, d, st, off)
-                head(st, 0, pieces // 2)
+                head(st, [near])
+            if k == n - 1:
+                for d in sides(st):
+                    ag_arrived(0, d, st, between[-2])
+                head(st, [aside])
             yield
         ag_chain(0, st, n)
         for d in sides(st):
             ag_arrived(0, d, st, far - 1)
-        head(st, pieces // 2, pieces)
+        head(st, rest)
         for k in range(n):
             rs_chain(1, st, k)
             yield

time: 98.9 us -> 102 us (1.031)
  Pallas kernels: 94.9 us -> 97.8 us
    pallas_call x1, Pallas kernels: 94.9 us -> 97.8 us  [shards(): pl.pallas_call(functools.partial(kernel, 1.0 / (patients * tasks * n_task...]
where the time goes in v1:
time: 102 us
  Pallas kernels  97.8 us (96%)
  between operations  2.33 us (2%)
    pallas_call x1, Pallas kernels, shards(): pl.pallas_call(functools.partial(kernel, 1.0 / (patients * tasks * n_task...  97.8 us

profile of v1, /device:TPU:1, one launch (start us, length us, event | category | flops | bytes accessed | tf_op | source)
XLA Modules:
  0.0 101.6 jit_solution(10837915622884714304)
XLA Ops:
  0.6 97.8 %shard_map.103 = (bf16[160,256]{1,0:T(8,128)(2,1)S(1)}, bf16[256,512]{1,0:T(8,128)(2,1)S(1)}, f32[1,1]{1,0:T(1,128)}) custom-call(bf16[160,256]{1,0:T(8,128)(2,1)} %bitcast.7, bf16[160,4096]{1,0:T(8,128)(2,1)} %pw_hbm.1, bf16[256,512]{1,0:T(8,128)(2,1)} %te_hbm.1, f32[8,256]{1,0:T(8,128)} %bitcast.8, s32[256,256]{1,0:T(8,128)} %bins_hbm.1, ...), custom_call_target="tpu_custom_call" | custom-call | flops 2400000000 | bytes 4000000 | tf_op jit(solution)/shard_map/pallas_call | solution.py:643
  98.4 0.6 copy.13
  99.1 0.9 convert_element_type.3

commit v2 on v0

--- a/solution.py
+++ b/solution.py
@@ -37,6 +37,7 @@
     hid_rows,
     pw,
     te,
+    te_t,
     bias,
     bins,
     cens,
@@ -323,7 +324,7 @@
         )
         total = None
         for h in range(2):
-            dots = lax.dot_general(zs, te[h], NT, preferred_element_type=F32)
+            dots = jnp.dot(zs, te_t[h], preferred_element_type=F32)
             edge = bins[h, span, :]
             alive = (1 - cens[h, span, :]).astype(F32)
             weight = wrow[span, :]
@@ -516,6 +517,11 @@
             yield
             if k == 1:
                 rs_sent(0, st)
+            if st == 0 and k == 0:
+                loads[2].wait()
+                pair[1].wait_recv()
+                for h in range(2):
+                    te_t[h] = te[h].T
             if st == 0 and k == 2:
                 for copy in pair:
                     copy.wait_send()
@@ -523,7 +529,7 @@
                     pw_copy(m).wait_send()
             if k == n - 1:
                 if st == 0:
-                    for i in range(1, 5):
+                    for i in range(2, 5):
                         loads[1 + i].wait()
                         pair[i].wait_recv()
                 for off in between[:-1]:
@@ -648,6 +654,7 @@
             pltpu.VMEM((2, rows, depth), BF16),
             pltpu.VMEM((2, depth, half), BF16),
             pltpu.VMEM((2, tasks, width), BF16),
+            pltpu.VMEM((2, width, tasks), BF16),
             pltpu.VMEM((2, pieces, tasks), F32),
             pltpu.VMEM((2, rows, tasks), jnp.int32),
             pltpu.VMEM((2, rows, tasks), jnp.int32),

time: 98.9 us -> 99.1 us (level)
  no operation moved by 1% of the time
where the time goes in v2:
time: 99.1 us; the launch traced here: 99 us
  Pallas kernels  95.2 us (96%)
  between operations  2.33 us (2%)
    pallas_call x1, Pallas kernels, shards(): pl.pallas_call(functools.partial(kernel, 1.0 / (patients * tasks * n_task...  95.2 us

profile of v2, /device:TPU:1, one launch (start us, length us, event | category | flops | bytes accessed | tf_op | source)
XLA Modules:
  0.0 99.0 jit_solution(3166126191314764126)
XLA Ops:
  0.6 95.2 %shard_map.103 = (bf16[160,256]{1,0:T(8,128)(2,1)S(1)}, bf16[256,512]{1,0:T(8,128)(2,1)S(1)}, f32[1,1]{1,0:T(1,128)}) custom-call(bf16[160,256]{1,0:T(8,128)(2,1)} %bitcast.7, bf16[160,4096]{1,0:T(8,128)(2,1)} %pw_hbm.1, bf16[256,512]{1,0:T(8,128)(2,1)} %te_hbm.1, f32[8,256]{1,0:T(8,128)} %bitcast.8, s32[256,256]{1,0:T(8,128)} %bins_hbm.1, ...), custom_call_target="tpu_custom_call" | custom-call | flops 2400000000 | bytes 4000000 | tf_op jit(solution)/shard_map/pallas_call | solution.py:641
  95.8 0.6 copy.13
  96.4 0.9 convert_element_type.3
